TPU v7x, 32 devices: a whole 2x2x4 slice. The times are simulated.
32 devices in a mesh: dp: 2 (over x), ctx: 16 (over z, y, core).
Axes of the slice: x: 2, y: 2, z: 4, core: 2. Of those that a mesh axis runs over, the one named last changes fastest.
Arguments:
- gate_outer: bfloat16 [2, 512, 2048], P('dp', None, 'ctx'), may hold values from -6 to 6
- gate_inner: bfloat16 [2, 512, 2048], P('dp', None, 'ctx'), may hold values from -6 to 6
- values_in: bfloat16 [2, 512, 2048], P('dp', None, 'ctx'), may hold values from -6 to 6
- cotangent: bfloat16 [2, 512, 2048], P('dp', None, 'ctx'), may hold values from -6 to 6
- filter_taps: bfloat16 [512, 2048], P(None, 'ctx'), may hold values from -2 to 2, as said below
- skip_gain: float32 [512], replicated, may hold values from 0.3 to 3
Outputs:
- hyena_result_array: bfloat16 [2, 512, 2048], P('dp', None, 'ctx')
- grad_outer: bfloat16 [2, 512, 2048], P('dp', None, 'ctx')
- grad_inner: bfloat16 [2, 512, 2048], P('dp', None, 'ctx')
- grad_values: bfloat16 [2, 512, 2048], P('dp', None, 'ctx')
- filter_grad: float32 [512, 2048], P(None, 'ctx')
Inputs may be any that keep to these rules, and one draw needn't show every extreme that they name: `filter_taps`: one filter of 2048 taps for each channel.
All inputs are finite; a program needn't handle non-finite values.
Results may differ from a plain program's by a relative error of at most 0.011.
Values may be sent and summed in bfloat16 or wider, within the bound.
A program may use at most 64 MiB of HBM per device.

v0:
```python
import math

import jax
import jax.numpy as jnp
from jax import lax
from jax.sharding import PartitionSpec as P

highest = lax.Precision.HIGHEST
inner_order = 128


def tables(order, count):
    rows = lax.broadcasted_iota(jnp.int32, (order, count), 0)
    cols = lax.broadcasted_iota(jnp.int32, (order, count), 1)
    angle = (rows * cols % order).astype(jnp.float32) * (2.0 * math.pi / order)
    return (jnp.cos(angle), jnp.sin(angle))


def twiddles(outer_order, total):
    rows = lax.broadcasted_iota(jnp.int32, (outer_order, inner_order), 0)
    cols = lax.broadcasted_iota(jnp.int32, (outer_order, inner_order), 1)
    angle = (rows * cols % total).astype(jnp.float32) * (2.0 * math.pi / total)
    return (jnp.cos(angle), jnp.sin(angle))


def forward_spectrum(signal):
    chans, seq = signal.shape
    outer_order = 2 * seq // inner_order
    half = outer_order // 2
    block_groups = signal.reshape(chans, half, inner_order)
    cos_p, sin_p = tables(outer_order, half)
    a_re = jnp.einsum("kn,cnm->ckm", cos_p, block_groups, precision=highest)
    a_im = -jnp.einsum("kn,cnm->ckm", sin_p, block_groups, precision=highest)
    tw_c, tw_s = twiddles(outer_order, outer_order * inner_order)
    b_re = a_re * tw_c + a_im * tw_s
    b_im = a_im * tw_c - a_re * tw_s
    cos_q, sin_q = tables(inner_order, inner_order)
    x_re = jnp.einsum("ckn,nm->ckm", b_re, cos_q, precision=highest) + jnp.einsum(
        "ckn,nm->ckm", b_im, sin_q, precision=highest
    )
    x_im = jnp.einsum("ckn,nm->ckm", b_im, cos_q, precision=highest) - jnp.einsum(
        "ckn,nm->ckm", b_re, sin_q, precision=highest
    )
    return (x_re, x_im)


def inverse_real_part(y_re, y_im):
    chans, outer_order, _ = y_re.shape
    half = outer_order // 2
    total = outer_order * inner_order
    cos_q, sin_q = tables(inner_order, inner_order)
    z_re = jnp.einsum("ckn,nm->ckm", y_re, cos_q, precision=highest) - jnp.einsum(
        "ckn,nm->ckm", y_im, sin_q, precision=highest
    )
    z_im = jnp.einsum("ckn,nm->ckm", y_im, cos_q, precision=highest) + jnp.einsum(
        "ckn,nm->ckm", y_re, sin_q, precision=highest
    )
    tw_c, tw_s = twiddles(outer_order, total)
    w_re = z_re * tw_c - z_im * tw_s
    w_im = z_im * tw_c + z_re * tw_s
    cos_p, sin_p = tables(outer_order, half)
    result = jnp.einsum("kn,ckm->cnm", cos_p, w_re, precision=highest) - jnp.einsum(
        "kn,ckm->cnm", sin_p, w_im, precision=highest
    )
    return (result * (1.0 / total)).reshape(chans, half * inner_order)


def on_device(gate_outer, gate_inner, values_in, cotangent, filter_taps, skip_gain):
    outer = gate_outer[0]
    inner = gate_inner[0]
    values = values_in[0]
    cotan = cotangent[0]
    chans_all, tok_dev = outer.shape
    ctx_count = lax.axis_size("ctx")
    dp_count = lax.axis_size("dp")
    seq = tok_dev * ctx_count
    norm_scale = 1.0 / math.sqrt(dp_count * seq)
    mixed = (inner.astype(jnp.float32) * values.astype(jnp.float32)).astype(jnp.bfloat16)
    back_in = (cotan.astype(jnp.float32) * outer.astype(jnp.float32)).astype(jnp.bfloat16)
    mixed_ch, back_ch, taps_ch = (
        lax.all_to_all(mixed, "ctx", split_axis=0, concat_axis=1, tiled=True),
        lax.all_to_all(back_in, "ctx", split_axis=0, concat_axis=1, tiled=True),
        lax.all_to_all(filter_taps, "ctx", split_axis=0, concat_axis=1, tiled=True),
    )
    h_re, h_im = forward_spectrum(taps_ch.astype(jnp.float32))
    u_re, u_im = forward_spectrum(mixed_ch.astype(jnp.float32))
    d_re, d_im = forward_spectrum(back_ch.astype(jnp.float32))
    conv_ch = inverse_real_part(u_re * h_re - u_im * h_im, u_re * h_im + u_im * h_re).astype(
        jnp.bfloat16
    )
    back_ch_out = inverse_real_part(h_re * d_re + h_im * d_im, h_re * d_im - h_im * d_re).astype(
        jnp.bfloat16
    )
    conv_seq, reverse_sweep_along_strand = (
        lax.all_to_all(conv_ch, "ctx", split_axis=1, concat_axis=0, tiled=True),
        lax.all_to_all(back_ch_out, "ctx", split_axis=1, concat_axis=0, tiled=True),
    )
    g_re = d_re * u_re + d_im * u_im
    g_im = d_im * u_re - d_re * u_im
    term = inverse_real_part(g_re, g_im)
    summed = lax.psum(term, "dp")
    filter_grad = lax.all_to_all(
        summed * norm_scale, "ctx", split_axis=1, concat_axis=0, tiled=True
    )
    gain = skip_gain[:, None]
    state = conv_seq.astype(jnp.float32) + gain * mixed.astype(jnp.float32)
    layer = (outer.astype(jnp.float32) * state).astype(jnp.bfloat16)
    g_outer = (cotan.astype(jnp.float32) * state).astype(jnp.bfloat16)
    g_mixed = reverse_sweep_along_strand.astype(jnp.float32) + gain * back_in.astype(jnp.float32)
    g_inner = (g_mixed * values.astype(jnp.float32)).astype(jnp.bfloat16)
    g_values = (g_mixed * inner.astype(jnp.float32)).astype(jnp.bfloat16)
    return (layer[None], g_outer[None], g_inner[None], g_values[None], filter_grad)


def solution(mesh):
    placed = (
        P("dp", None, "ctx"),
        P("dp", None, "ctx"),
        P("dp", None, "ctx"),
        P("dp", None, "ctx"),
        P(None, "ctx"),
        P(),
    )
    return jax.shard_map(
        on_device,
        mesh=mesh,
        in_specs=placed,
        out_specs=(
            P("dp", None, "ctx"),
            P("dp", None, "ctx"),
            P("dp", None, "ctx"),
            P("dp", None, "ctx"),
            P(None, "ctx"),
        ),
        check_vma=False,
    )
```

profile of v0, /device:TPU:0, one launch (start us, length us, event | category | flops | bytes accessed | tf_op | source)
XLA Modules:
  0.0 122.4 jit_solution(11661278349426232779)
XLA Ops:
  7.2 1.9 %fusion.38 = (bf16[1,512,128]{2,1,0:T(8,128)(2,1)}, bf16[1,512,128]{2,1,0:T(8,128)(2,1)}) fusion(bf16[1,512,128]{2,1,0:T(8,128)(2,1)} %param.8, bf16[1,512,128]{2,1,0:T(8,128)(2,1)} %param.7, bf16[1,512,128]{2,1,0:T(8,128)(2,1)} %param.6, bf16[1,512,128]{2,1,0:T(8,128)(2,1)} %param.9), kind=kLoop, calls=%fused_computation.76 | loop fusion | flops 524288 | bytes 786432 | tf_op jit(solution)/shard_map/convert_element_type | solution.py:78
  9.0 7.4 %all-to-all-start = ((bf16[16,32,128]{2,1,0:T(8,128)(2,1)}), bf16[16,32,128]{2,1,0:T(8,128)(2,1)S(1)}, u32[]{:S(2)}, u32[]{:S(2)}) async-start(bf16[16,32,128]{2,1,0:T(8,128)(2,1)} %bitcast), calls=%async_computation | async-start | bytes 262144 | tf_op jit(solution)/shard_map/all_to_all | solution.py:81
  16.4 0.1 fusion.154
  16.5 7.8 %all-to-all-done = bf16[16,32,128]{2,1,0:T(8,128)(2,1)S(1)} async-done(((bf16[16,32,128]{2,1,0:T(8,128)(2,1)}), bf16[16,32,128]{2,1,0:T(8,128)(2,1)S(1)}, u32[]{:S(2)}, u32[]{:S(2)}) %all-to-all-start) | async-done | bytes 131104 | tf_op jit(solution)/shard_map/all_to_all | solution.py:81
  24.4 3.5 %all-to-all-start.1 = ((bf16[16,32,128]{2,1,0:T(8,128)(2,1)}), bf16[16,32,128]{2,1,0:T(8,128)(2,1)S(1)}, u32[]{:S(2)}, u32[]{:S(2)}) async-start(bf16[16,32,128]{2,1,0:T(8,128)(2,1)} %bitcast.8), calls=%async_computation.1 | async-start | bytes 262144 | tf_op jit(solution)/shard_map/all_to_all | solution.py:83
  27.9 0.5 convolution_bitcast_fusion.1
  28.4 0.5 fusion.1
  28.8 0.8 fusion.55
  29.7 0.8 fusion.54
  30.5 5.3 %all-to-all-done.1 = bf16[16,32,128]{2,1,0:T(8,128)(2,1)S(1)} async-done(((bf16[16,32,128]{2,1,0:T(8,128)(2,1)}), bf16[16,32,128]{2,1,0:T(8,128)(2,1)S(1)}, u32[]{:S(2)}, u32[]{:S(2)}) %all-to-all-start.1) | async-done | bytes 131104 | tf_op jit(solution)/shard_map/all_to_all | solution.py:83
  35.8 3.7 %all-to-all-start.3 = ((bf16[16,32,128]{2,1,0:T(8,128)(2,1)}), bf16[16,32,128]{2,1,0:T(8,128)(2,1)S(1)}, u32[]{:S(2)}, u32[]{:S(2)}) async-start(bf16[16,32,128]{2,1,0:T(8,128)(2,1)} %bitcast.15), calls=%async_computation.3 | async-start | bytes 262144 | tf_op jit(solution)/shard_map/all_to_all | solution.py:82
  39.5 0.5 convolution_negate_fusion.1
  40.0 0.5 fusion.61
  40.4 1.6 %fusion.13 = f32[32,32,128]{2,1,0:T(8,128)} fusion(f32[32,32,128]{2,0,1:T(8,128)S(1)} %convolution_negate_fusion.1, f32[32,32,128]{2,0,1:T(8,128)S(1)} %fusion.61, f32[32,128]{1,0:T(8,128)S(1)} %get-tuple-element.21, f32[32,128]{1,0:T(8,128)S(1)} %get-tuple-element.22), kind=kOutput, calls=%fused_computation.33 | convolution fusion | flops 201949184 | bytes 1605632 | tf_op jit(solution)/shard_map/ckn,nm->ckm/dot_general | solution.py:38
  42.1 1.6 %fusion.9 = f32[32,32,128]{2,1,0:T(8,128)} fusion(f32[32,32,128]{2,0,1:T(8,128)S(1)} %fusion.61, f32[32,32,128]{2,0,1:T(8,128)S(1)} %convolution_negate_fusion.1, f32[32,128]{1,0:T(8,128)S(1)} %get-tuple-element.21, f32[32,128]{1,0:T(8,128)S(1)} %get-tuple-element.22), kind=kOutput, calls=%fused_computation.29 | convolution fusion | flops 201949184 | bytes 1605632 | tf_op jit(solution)/shard_map/ckn,nm->ckm/dot_general | solution.py:41
  43.7 3.5 %all-to-all-done.3 = bf16[16,32,128]{2,1,0:T(8,128)(2,1)S(1)} async-done(((bf16[16,32,128]{2,1,0:T(8,128)(2,1)}), bf16[16,32,128]{2,1,0:T(8,128)(2,1)S(1)}, u32[]{:S(2)}, u32[]{:S(2)}) %all-to-all-start.3) | async-done | bytes 131104 | tf_op jit(solution)/shard_map/all_to_all | solution.py:82
  47.2 0.5 fusion
  47.7 0.5 convolution_bitcast_fusion
  48.2 0.8 fusion.56
  49.0 0.8 fusion.57
  49.8 0.8 convolution_subtract_fusion.5
  50.6 0.8 convolution_add_fusion.2
  51.5 0.0 copy-start.1
  51.5 0.8 convolution_add_fusion.5
  52.3 0.2 copy-done.1
  52.5 0.8 convolution_add_fusion.4
  53.3 0.2 copy-done
  53.6 0.8 convolution_subtract_fusion.4
  54.4 1.1 multiply_add_fusion
  55.5 0.8 fusion.90
  56.3 0.8 fusion.92
  57.1 1.1 convolution_add_fusion.1
  58.2 0.8 convolution_subtract_fusion.1
  59.0 0.5 fusion.25
  59.5 0.5 fusion.7
  60.0 0.7 copy.22
  60.7 3.5 %all-to-all-start.4 = ((bf16[32,16,128]{2,0,1:T(8,128)(2,1)}), bf16[32,16,128]{2,0,1:T(8,128)(2,1)S(1)}, u32[]{:S(2)}, u32[]{:S(2)}) async-start(bf16[32,16,128]{2,0,1:T(8,128)(2,1)} %copy.22), calls=%async_computation.4 | async-start | bytes 262144 | tf_op jit(solution)/shard_map/all_to_all | solution.py:96
  64.3 0.0 all-reduce.2.cloned.1.call-start
  64.3 0.8 fusion.96
  65.1 0.8 fusion.98
  65.9 0.8 convolution_add_fusion.3
  66.8 0.8 convolution_subtract_fusion.3
  67.6 0.8 fusion.86
  68.4 0.8 fusion.88
  69.2 0.8 convolution_add_fusion
  70.1 0.8 convolution_subtract_fusion
  70.9 0.5 fusion.18
  71.4 0.5 fusion.2
  71.9 0.8 copy.52
  72.7 0.0 all-reduce.2.cloned.1.call-update
  72.7 0.5 fusion.32
  73.2 0.5 fusion.8
  73.7 0.7 copy.20
  74.4 0.0 all-to-all-done.4
  74.4 6.0 %all-to-all-start.2 = ((bf16[32,16,128]{2,0,1:T(8,128)(2,1)}), bf16[32,16,128]{2,0,1:T(8,128)(2,1)S(1)}, u32[]{:S(2)}, u32[]{:S(2)}) async-start(bf16[32,16,128]{2,0,1:T(8,128)(2,1)} %copy.20), calls=%async_computation.2 | async-start | bytes 262144 | tf_op jit(solution)/shard_map/all_to_all | solution.py:95
  80.4 17.0 %all-reduce.2.cloned.1.call-done = f32[32,2048]{1,0:T(8,128)} async-done(((f32[32,2048]{1,0:T(8,128)}), f32[32,2048]{1,0:T(8,128)}) %all-reduce.2.cloned.1.call-update) | async-done | bytes 262160 | tf_op jit(solution)/shard_map/psum | solution.py:101
  97.4 1.7 %copy_bitcast_fusion.1 = f32[32,16,128]{2,0,1:T(8,128)} fusion(f32[32,2048]{1,0:T(8,128)} %all-reduce.2.cloned.1.call-done), kind=kLoop, calls=%fused_computation.81 | loop fusion | flops 65536 | bytes 524288 | tf_op jit(solution)/shard_map/all_to_all | solution.py:102
  99.1 0.0 all-to-all-done.2
  99.1 5.8 %all-to-all-start.5 = ((f32[32,16,128]{2,0,1:T(8,128)}), f32[32,16,128]{2,0,1:T(8,128)S(1)}, u32[]{:S(2)}, u32[]{:S(2)}) async-start(f32[32,16,128]{2,0,1:T(8,128)} %copy_bitcast_fusion.1), calls=%async_computation.5 | async-start | bytes 524288 | tf_op jit(solution)/shard_map/all_to_all | solution.py:102
  104.8 0.0 copy-done.6
  104.9 0.0 copy-done.2
  104.9 2.0 %fusion.37 = (bf16[1,512,128]{2,1,0:T(8,128)(2,1)}, bf16[1,512,128]{2,1,0:T(8,128)(2,1)}, bf16[1,512,128]{2,1,0:T(8,128)(2,1)}, bf16[1,512,128]{2,1,0:T(8,128)(2,1)}) fusion(bf16[1,512,128]{2,1,0:T(8,128)(2,1)S(1)} %copy-done.2, bf16[1,512,128]{2,1,0:T(8,128)(2,1)} %get-tuple-element.24, bf16[32,16,128]{2,0,1:T(8,128)(2,1)S(1)} %all-to-all-done.4, ...), kind=kLoop, calls=%fused_computation.75 | loop fusion | flops 1310720 | bytes 1574912 | tf_op jit(solution)/shard_map/convert_element_type | solution.py:111
  106.9 8.0 %all-to-all-done.5 = f32[32,16,128]{2,0,1:T(8,128)S(1)} async-done(((f32[32,16,128]{2,0,1:T(8,128)}), f32[32,16,128]{2,0,1:T(8,128)S(1)}, u32[]{:S(2)}, u32[]{:S(2)}) %all-to-all-start.5) | async-done | bytes 262176 | tf_op jit(solution)/shard_map/all_to_all | solution.py:102
  114.9 0.7 copy.55
  (9 shorter events, 0.0 us)
Async XLA Ops:
  9.0 15.3 %all-to-all-start = ((bf16[16,32,128]{2,1,0:T(8,128)(2,1)}), bf16[16,32,128]{2,1,0:T(8,128)(2,1)S(1)}, u32[]{:S(2)}, u32[]{:S(2)}) async-start(bf16[16,32,128]{2,1,0:T(8,128)(2,1)} %bitcast), calls=%async_computation | async-start | bytes 262144 | tf_op jit(solution)/shard_map/all_to_all | solution.py:81
  24.4 11.4 %all-to-all-start.1 = ((bf16[16,32,128]{2,1,0:T(8,128)(2,1)}), bf16[16,32,128]{2,1,0:T(8,128)(2,1)S(1)}, u32[]{:S(2)}, u32[]{:S(2)}) async-start(bf16[16,32,128]{2,1,0:T(8,128)(2,1)} %bitcast.8), calls=%async_computation.1 | async-start | bytes 262144 | tf_op jit(solution)/shard_map/all_to_all | solution.py:83
  35.8 11.4 %all-to-all-start.3 = ((bf16[16,32,128]{2,1,0:T(8,128)(2,1)}), bf16[16,32,128]{2,1,0:T(8,128)(2,1)S(1)}, u32[]{:S(2)}, u32[]{:S(2)}) async-start(bf16[16,32,128]{2,1,0:T(8,128)(2,1)} %bitcast.15), calls=%async_computation.3 | async-start | bytes 262144 | tf_op jit(solution)/shard_map/all_to_all | solution.py:82
  51.5 1.0 copy-start.1
  52.5 1.0 copy-start
  60.7 13.7 %all-to-all-start.4 = ((bf16[32,16,128]{2,0,1:T(8,128)(2,1)}), bf16[32,16,128]{2,0,1:T(8,128)(2,1)S(1)}, u32[]{:S(2)}, u32[]{:S(2)}) async-start(bf16[32,16,128]{2,0,1:T(8,128)(2,1)} %copy.22), calls=%async_computation.4 | async-start | bytes 262144 | tf_op jit(solution)/shard_map/all_to_all | solution.py:96
  64.3 33.1 %all-reduce.2.cloned.1.call-start = ((), (), s32[]{:S(2)}) async-start(), calls=%async_computation.6 | async-start | bytes 524288 | tf_op jit(solution)/shard_map/psum | solution.py:101
  74.4 24.6 %all-to-all-start.2 = ((bf16[32,16,128]{2,0,1:T(8,128)(2,1)}), bf16[32,16,128]{2,0,1:T(8,128)(2,1)S(1)}, u32[]{:S(2)}, u32[]{:S(2)}) async-start(bf16[32,16,128]{2,0,1:T(8,128)(2,1)} %copy.20), calls=%async_computation.2 | async-start | bytes 262144 | tf_op jit(solution)/shard_map/all_to_all | solution.py:95
  97.4 7.5 %copy-start.6 = (f32[512]{0:T(512)S(1)}, f32[512]{0:T(512)}, u32[]{:S(2)}) copy-start(f32[512]{0:T(512)} %param.11) | copy-start | bytes 6148
  99.1 5.8 %copy-start.2 = (bf16[1,512,128]{2,1,0:T(8,128)(2,1)S(1)}, bf16[1,512,128]{2,1,0:T(8,128)(2,1)}, u32[]{:S(2)}) copy-start(bf16[1,512,128]{2,1,0:T(8,128)(2,1)} %param.7) | copy-start | bytes 393220
  99.1 5.8 %copy-start.3 = (bf16[1,512,128]{2,1,0:T(8,128)(2,1)S(1)}, bf16[1,512,128]{2,1,0:T(8,128)(2,1)}, u32[]{:S(2)}) copy-start(bf16[1,512,128]{2,1,0:T(8,128)(2,1)} %param.8) | copy-start | bytes 393220
  99.1 5.8 %copy-start.4 = (bf16[1,512,128]{2,1,0:T(8,128)(2,1)S(1)}, bf16[1,512,128]{2,1,0:T(8,128)(2,1)}, u32[]{:S(2)}) copy-start(bf16[1,512,128]{2,1,0:T(8,128)(2,1)} %param.6) | copy-start | bytes 393220
  99.1 5.8 %copy-start.5 = (bf16[1,512,128]{2,1,0:T(8,128)(2,1)S(1)}, bf16[1,512,128]{2,1,0:T(8,128)(2,1)}, u32[]{:S(2)}) copy-start(bf16[1,512,128]{2,1,0:T(8,128)(2,1)} %param.9) | copy-start | bytes 393220
  99.1 15.8 %all-to-all-start.5 = ((f32[32,16,128]{2,0,1:T(8,128)}), f32[32,16,128]{2,0,1:T(8,128)S(1)}, u32[]{:S(2)}, u32[]{:S(2)}) async-start(f32[32,16,128]{2,0,1:T(8,128)} %copy_bitcast_fusion.1), calls=%async_computation.5 | async-start | bytes 524288 | tf_op jit(solution)/shard_map/all_to_all | solution.py:102
Sparse Core Ops, SparseCore 0:
  72.8 24.4 all-reduce.1
where the time goes:
time: 123 us; the launch traced here: 122 us
  waiting for transfers between devices  41.6 us (34%)
  starting transfers between devices  29.9 us (24%)
  matrix products  27.6 us (22%)
  between operations  14.4 us (12%)
  other arithmetic  5.64 us (5%)
  local copies, waits for them, and re-layouts  3.31 us (3%)
    psum x1, waiting for transfers between devices, on_device(): summed = lax.psum(term, 'dp')  17 us
    all_to_all x1, waiting for transfers between devices, on_device(): lax.all_to_all(summed * norm_scale, 'ctx', split_axis=1, concat_axis=0, t...  8 us
    all_to_all x1, waiting for transfers between devices, on_device(): lax.all_to_all(mixed, 'ctx', split_axis=0, concat_axis=1, tiled=True)  7.85 us
    all_to_all x1, starting transfers between devices, on_device(): lax.all_to_all(mixed, 'ctx', split_axis=0, concat_axis=1, tiled=True)  7.39 us
    all_to_all x1, starting transfers between devices, on_device(): lax.all_to_all(conv_ch, 'ctx', split_axis=1, concat_axis=0, tiled=True)  5.96 us
    all_to_all x1, starting transfers between devices, on_device(): lax.all_to_all(summed * norm_scale, 'ctx', split_axis=1, concat_axis=0, t...  5.76 us
    all_to_all x1, waiting for transfers between devices, on_device(): lax.all_to_all(filter_taps, 'ctx', split_axis=0, concat_axis=1, tiled=True)  5.28 us
    all_to_all x1, starting transfers between devices, on_device(): lax.all_to_all(back_in, 'ctx', split_axis=0, concat_axis=1, tiled=True)  3.69 us
  transfers between devices with their start and end apart: 7, of which 5 were waited for; matrix products, arithmetic and copies ran while one was open for 17% of the time, Pallas kernels for 0%

commit v1 on v0

--- a/solution.py
+++ b/solution.py
@@ -1,12 +1,19 @@
+import functools
 import math
 
 import jax
 import jax.numpy as jnp
+import numpy as np
 from jax import lax
+from jax.experimental import pallas as pl
+from jax.experimental.pallas import tpu as pltpu
 from jax.sharding import PartitionSpec as P
 
 highest = lax.Precision.HIGHEST
 inner_order = 128
+MESH = pl.DeviceIdType.MESH
+F32 = jnp.float32
+BF16 = jnp.bfloat16
 
 
 def tables(order, count):
@@ -65,18 +72,11 @@
     return (result * (1.0 / total)).reshape(chans, half * inner_order)
 
 
-def on_device(gate_outer, gate_inner, values_in, cotangent, filter_taps, skip_gain):
-    outer = gate_outer[0]
-    inner = gate_inner[0]
-    values = values_in[0]
-    cotan = cotangent[0]
-    chans_all, tok_dev = outer.shape
+def general_exchange(mixed, back_in, filter_taps):
     ctx_count = lax.axis_size("ctx")
     dp_count = lax.axis_size("dp")
-    seq = tok_dev * ctx_count
+    seq = mixed.shape[1] * ctx_count
     norm_scale = 1.0 / math.sqrt(dp_count * seq)
-    mixed = (inner.astype(jnp.float32) * values.astype(jnp.float32)).astype(jnp.bfloat16)
-    back_in = (cotan.astype(jnp.float32) * outer.astype(jnp.float32)).astype(jnp.bfloat16)
     mixed_ch, back_ch, taps_ch = (
         lax.all_to_all(mixed, "ctx", split_axis=0, concat_axis=1, tiled=True),
         lax.all_to_all(back_in, "ctx", split_axis=0, concat_axis=1, tiled=True),
@@ -91,7 +91,7 @@
     back_ch_out = inverse_real_part(h_re * d_re + h_im * d_im, h_re * d_im - h_im * d_re).astype(
         jnp.bfloat16
     )
-    conv_seq, reverse_sweep_along_strand = (
+    conv_seq, back_seq = (
         lax.all_to_all(conv_ch, "ctx", split_axis=1, concat_axis=0, tiled=True),
         lax.all_to_all(back_ch_out, "ctx", split_axis=1, concat_axis=0, tiled=True),
     )
@@ -102,14 +102,298 @@
     filter_grad = lax.all_to_all(
         summed * norm_scale, "ctx", split_axis=1, concat_axis=0, tiled=True
     )
+    return conv_seq, back_seq, filter_grad
+
+
+def two_parts(table):
+    high = table.astype(np.float32).astype(BF16)
+    low = (table - high.astype(np.float64)).astype(np.float32).astype(BF16)
+    return np.stack([np.asarray(high), np.asarray(low)])
+
+
+@functools.lru_cache(maxsize=None)
+def kernel_tables(blocks, group, width):
+    total = 2 * blocks * width
+    n = np.arange(blocks)
+    angle = 2.0 * np.pi * ((np.outer(2 * n + 1, n)) % (4 * blocks)) / (4 * blocks)
+    unit = np.eye(group)
+    outer_f = np.concatenate([np.kron(np.cos(angle), unit), np.kron(-np.sin(angle), unit)], axis=0)
+    outer_i = outer_f.T * (2.0 / total)
+    m = np.arange(width)
+    angle_in = 2.0 * np.pi * (np.outer(m, m) % width) / width
+    c, s = np.cos(angle_in), np.sin(angle_in)
+    inner_f = np.block([[c, -s], [s, c]])
+    inner_i = np.block([[c, s], [-s, c]])
+    angle_tw = 2.0 * np.pi * np.outer(2 * n + 1, m) / (2.0 * total)
+    tw = np.stack([np.cos(angle_tw), np.sin(angle_tw)])
+    tw = np.repeat(tw, group, axis=1).astype(np.float32)
+    return two_parts(outer_f), two_parts(outer_i), two_parts(inner_f), two_parts(inner_i), tw
+
+
+def dot(a, b):
+    return jnp.dot(a, b, preferred_element_type=F32)
+
+
+def split(x):
+    high = x.astype(BF16)
+    return high, (x - high.astype(F32)).astype(BF16)
+
+
+def kernel(
+    dp_count,
+    ctx_count,
+    outer_ref,
+    inner_ref,
+    values_ref,
+    cotan_ref,
+    taps_ref,
+    outer_f_hbm,
+    outer_i_hbm,
+    inner_f_hbm,
+    inner_i_hbm,
+    tw_hbm,
+    conv_out,
+    back_out,
+    grad_out,
+    mixed,
+    back_in,
+    recv_u,
+    recv_d,
+    recv_h,
+    sent_conv,
+    sent_back,
+    sent_grad,
+    outer_f,
+    outer_i,
+    inner_f,
+    inner_i,
+    tw,
+    table_sems,
+    send_sems,
+    recv_sems,
+):
+    ranks = dp_count * ctx_count
+    chans, width = mixed.shape
+    group = chans // ranks
+    rows = ctx_count * group
+    my_dp = lax.axis_index("dp")
+    my_ctx = lax.axis_index("ctx")
+    me = my_dp * ctx_count + my_ctx
+
+    barrier = pltpu.get_barrier_semaphore()
+
+    def greet(i, carry):
+        peer = lax.rem(me + i, ranks)
+        pl.semaphore_signal(
+            barrier,
+            inc=1,
+            device_id=(peer // ctx_count, lax.rem(peer, ctx_count)),
+            device_id_type=MESH,
+        )
+        return carry
+
+    lax.fori_loop(1, ranks, greet, 0)
+
+    table_copies = [
+        pltpu.make_async_copy(src, dst, table_sems.at[i])
+        for i, (src, dst) in enumerate(
+            [
+                (outer_f_hbm, outer_f),
+                (inner_f_hbm, inner_f),
+                (tw_hbm, tw),
+                (inner_i_hbm, inner_i),
+                (outer_i_hbm, outer_i),
+            ]
+        )
+    ]
+    for copy in table_copies:
+        copy.start()
+
+    mixed[...] = (inner_ref[...].astype(F32) * values_ref[...].astype(F32)).astype(BF16)
+    back_in[...] = (cotan_ref[...].astype(F32) * outer_ref[...].astype(F32)).astype(BF16)
+    pl.semaphore_wait(barrier, ranks - 1)
+
+    def chunk(ref, index):
+        return ref.at[pl.ds(pl.multiple_of(index * group, group), group)]
+
+    def to_peer(src, dst, which, peer):
+        return pltpu.make_async_remote_copy(
+            src_ref=src,
+            dst_ref=dst,
+            send_sem=send_sems.at[which],
+            recv_sem=recv_sems.at[which],
+            device_id=(peer // ctx_count, lax.rem(peer, ctx_count)),
+            device_id_type=MESH,
+        )
+
+    def send_taps(i, carry):
+        ctx = lax.rem(my_ctx + i, ctx_count)
+        peer = my_dp * ctx_count + ctx
+        to_peer(chunk(taps_ref, peer), chunk(recv_h, my_ctx), 0, peer).start()
+        return carry
+
+    def send_mixed(i, carry):
+        peer = lax.rem(me + i, ranks)
+        to_peer(chunk(mixed, peer), chunk(recv_u, me), 1, peer).start()
+        return carry
+
+    def send_back(i, carry):
+        peer = lax.rem(me + i, ranks)
+        to_peer(chunk(back_in, peer), chunk(recv_d, me), 2, peer).start()
+        return carry
+
+    lax.fori_loop(1, ctx_count, send_taps, 0)
+    lax.fori_loop(1, ranks, send_mixed, 0)
+    lax.fori_loop(1, ranks, send_back, 0)
+    pltpu.make_async_copy(chunk(taps_ref, me), chunk(recv_h, my_ctx), recv_sems.at[0]).start()
+    pltpu.make_async_copy(chunk(mixed, me), chunk(recv_u, me), recv_sems.at[1]).start()
+    pltpu.make_async_copy(chunk(back_in, me), chunk(recv_d, me), recv_sems.at[2]).start()
+
+    def arrived(ref, which):
+        pltpu.make_async_copy(ref, ref, recv_sems.at[which]).wait()
+
+    def spectra(signals):
+        count = len(signals)
+        side = jnp.concatenate(signals, axis=1)
+        a = dot(outer_f[0], side) + dot(outer_f[1], side)
+        parts = []
+        for s in range(count):
+            re = a[:rows, s * width : (s + 1) * width]
+            im = a[rows:, s * width : (s + 1) * width]
+            parts.append(
+                jnp.concatenate([re * tw[0] + im * tw[1], im * tw[0] - re * tw[1]], axis=1)
+            )
+        high, low = split(jnp.concatenate(parts, axis=0))
+        x = dot(high, inner_f[0]) + (dot(high, inner_f[1]) + dot(low, inner_f[0]))
+        return [
+            (x[s * rows : (s + 1) * rows, :width], x[s * rows : (s + 1) * rows, width:])
+            for s in range(count)
+        ]
+
+    def signals_of(products):
+        count = len(products)
+        high, low = split(
+            jnp.concatenate([jnp.concatenate([re, im], axis=1) for re, im in products], axis=0)
+        )
+        z = dot(high, inner_i[0]) + (dot(high, inner_i[1]) + dot(low, inner_i[0]))
+        parts = []
+        for s in range(count):
+            re = z[s * rows : (s + 1) * rows, :width]
+            im = z[s * rows : (s + 1) * rows, width:]
+            parts.append(
+                jnp.concatenate([re * tw[0] - im * tw[1], im * tw[0] + re * tw[1]], axis=0)
+            )
+        high, low = split(jnp.concatenate(parts, axis=1))
+        y = dot(outer_i[0], high) + (dot(outer_i[1], high) + dot(outer_i[0], low))
+        return [y[:, s * width : (s + 1) * width] for s in range(count)]
+
+    def times(a, b):
+        return a[0] * b[0] - a[1] * b[1], a[0] * b[1] + a[1] * b[0]
+
+    def times_conj(a, b):
+        return a[0] * b[0] + a[1] * b[1], a[1] * b[0] - a[0] * b[1]
+
+    def return_sequences(src, dst, which):
+        def step(i, carry):
+            peer = lax.rem(me + i, ranks)
+            to_peer(chunk(src, peer), chunk(dst, me), which, peer).start()
+            return carry
+
+        lax.fori_loop(1, ranks, step, 0)
+        pltpu.make_async_copy(chunk(src, me), chunk(dst, me), recv_sems.at[which]).start()
+
+    arrived(recv_h, 0)
+    arrived(recv_u, 1)
+    for copy in table_copies:
+        copy.wait()
+    spec = spectra(
+        [recv_h[...]] + [recv_u[s * rows : (s + 1) * rows] for s in range(dp_count)]
+    )
+    spec_h, spec_u = spec[0], spec[1:]
+    for s, y in enumerate(signals_of([times(u, spec_h) for u in spec_u])):
+        sent_conv[s * rows : (s + 1) * rows] = y.astype(BF16)
+    return_sequences(sent_conv, conv_out, 3)
+
+    arrived(recv_d, 2)
+    spec_d = spectra([recv_d[s * rows : (s + 1) * rows] for s in range(dp_count)])
+    for s, y in enumerate(signals_of([times_conj(d, spec_h) for d in spec_d])):
+        sent_back[s * rows : (s + 1) * rows] = y.astype(BF16)
+    return_sequences(sent_back, back_out, 4)
+
+    terms = [times_conj(d, u) for d, u in zip(spec_d, spec_u)]
+    term = (sum(t[0] for t in terms), sum(t[1] for t in terms))
+    norm_scale = 1.0 / math.sqrt(dp_count * ctx_count * width)
+    sent_grad[...] = (signals_of([term])[0] * norm_scale).astype(BF16)
+
+    def send_grad(i, carry):
+        peer = lax.rem(me + i, ranks)
+        to_peer(chunk(sent_grad, lax.rem(peer, ctx_count)), chunk(grad_out, me), 5, peer).start()
+        return carry
+
+    lax.fori_loop(1, ranks, send_grad, 0)
+    pltpu.make_async_copy(chunk(sent_grad, my_ctx), chunk(grad_out, me), recv_sems.at[5]).start()
+
+    arrived(conv_out, 3)
+    arrived(back_out, 4)
+    arrived(grad_out, 5)
+    for which, count in ((0, ctx_count), (1, ranks), (2, ranks), (3, ranks), (4, ranks), (5, ranks)):
+        part = mixed.at[pl.ds(0, (count - 1) * group)]
+        pltpu.make_async_copy(part, part, send_sems.at[which]).wait()
+
+
+def kernel_exchange(outer, inner, values, cotan, filter_taps):
+    ctx_count = lax.axis_size("ctx")
+    dp_count = lax.axis_size("dp")
+    chans, width = outer.shape
+    group = chans // (dp_count * ctx_count)
+    rows = ctx_count * group
+    constants = kernel_tables(ctx_count, group, width)
+    vmem = pl.BlockSpec(memory_space=pltpu.VMEM)
+    anywhere = pl.BlockSpec(memory_space=pl.ANY)
+    local = jax.ShapeDtypeStruct((chans, width), BF16)
+    signal = pltpu.VMEM((chans, width), BF16)
+    one = pltpu.VMEM((rows, width), BF16)
+    return pl.pallas_call(
+        functools.partial(kernel, dp_count, ctx_count),
+        out_shape=(local, local, local),
+        in_specs=[vmem] * 5 + [anywhere] * 5,
+        out_specs=(vmem, vmem, vmem),
+        scratch_shapes=[signal, signal, signal, signal, one, signal, signal, one]
+        + [pltpu.VMEM(t.shape, t.dtype) for t in constants]
+        + [
+            pltpu.SemaphoreType.DMA((5,)),
+            pltpu.SemaphoreType.DMA((6,)),
+            pltpu.SemaphoreType.DMA((6,)),
+        ],
+        compiler_params=pltpu.CompilerParams(
+            collective_id=0, has_side_effects=True, vmem_limit_bytes=48 * 1024 * 1024
+        ),
+        cost_estimate=pl.CostEstimate(
+            flops=2_000_000_000, bytes_accessed=4_000_000, transcendentals=0
+        ),
+    )(outer, inner, values, cotan, filter_taps, *[jnp.asarray(t) for t in constants])
+
+
+def on_device(gate_outer, gate_inner, values_in, cotangent, filter_taps, skip_gain):
+    outer = gate_outer[0]
+    inner = gate_inner[0]
+    values = values_in[0]
+    cotan = cotangent[0]
+    ranks = lax.axis_size("ctx") * lax.axis_size("dp")
+    mixed = (inner.astype(F32) * values.astype(F32)).astype(BF16)
+    back_in = (cotan.astype(F32) * outer.astype(F32)).astype(BF16)
+    if outer.shape[0] % (16 * ranks) == 0 and outer.shape[1] == inner_order:
+        conv_seq, back_seq, filter_grad = kernel_exchange(outer, inner, values, cotan, filter_taps)
+    else:
+        conv_seq, back_seq, filter_grad = general_exchange(mixed, back_in, filter_taps)
     gain = skip_gain[:, None]
-    state = conv_seq.astype(jnp.float32) + gain * mixed.astype(jnp.float32)
-    layer = (outer.astype(jnp.float32) * state).astype(jnp.bfloat16)
-    g_outer = (cotan.astype(jnp.float32) * state).astype(jnp.bfloat16)
-    g_mixed = reverse_sweep_along_strand.astype(jnp.float32) + gain * back_in.astype(jnp.float32)
-    g_inner = (g_mixed * values.astype(jnp.float32)).astype(jnp.bfloat16)
-    g_values = (g_mixed * inner.astype(jnp.float32)).astype(jnp.bfloat16)
-    return (layer[None], g_outer[None], g_inner[None], g_values[None], filter_grad)
+    state = conv_seq.astype(F32) + gain * mixed.astype(F32)
+    layer = (outer.astype(F32) * state).astype(BF16)
+    g_outer = (cotan.astype(F32) * state).astype(BF16)
+    g_mixed = back_seq.astype(F32) + gain * back_in.astype(F32)
+    g_inner = (g_mixed * values.astype(F32)).astype(BF16)
+    g_values = (g_mixed * inner.astype(F32)).astype(BF16)
+    return (layer[None], g_outer[None], g_inner[None], g_values[None], filter_grad.astype(F32))
 
 
 def solution(mesh):

time: 123 us -> 40.7 us (0.33)
  waiting for transfers between devices: 41.6 us -> 0 us
  starting transfers between devices: 29.9 us -> 0 us
  Pallas kernels: 0 us -> 27.7 us
  matrix products: 27.6 us -> 0 us
  between operations: 14.4 us -> 0.67 us
  local copies, waits for them, and re-layouts: 3.31 us -> 10.1 us
  other arithmetic: 5.64 us -> 1.74 us
    all_to_all x6 -> x0, starting transfers between devices: 29.8 us -> none  [the longest x1 7.39 us: on_device(): lax.all_to_all(mixed, 'ctx', split_axis=0, concat_axis=1, tiled=True)]
    pallas_call x0 -> x1, Pallas kernels: none -> 27.7 us  [kernel_exchange(): pl.pallas_call(functools.partial(kernel, dp_count, ctx_count), out_shape=...]
    dot_general x36 -> x0, matrix products: 27.6 us -> none  [the longest x3 3.27 us: forward_spectrum(): jnp.einsum('ckn,nm->ckm', b_re, cos_q, precision=highest)]
    all_to_all x6 -> x0, waiting for transfers between devices: 24.7 us -> none  [the longest x1 8 us: on_device(): lax.all_to_all(summed * norm_scale, 'ctx', split_axis=1, concat_axis=0, t...]
    psum x1 -> x0, waiting for transfers between devices: 17 us -> none  [on_device(): summed = lax.psum(term, 'dp')]
    unnamed x16 -> x22, local copies, waits for them, and re-layouts: 1.93 us -> 10.1 us
    convert_element_type x2 -> x1, other arithmetic: 3.86 us -> 0.72 us  [on_device(): filter_grad.astype(F32)]
    all_to_all x1 -> x0, other arithmetic: 1.69 us -> none  [on_device(): lax.all_to_all(summed * norm_scale, 'ctx', split_axis=1, concat_axis=0, t...]
  transfers between devices with their start and end apart: 7 -> 0, of which waited for: 5 -> 0; matrix products, arithmetic and copies ran while one was open for 17% -> 0% of each run, Pallas kernels for 0% -> 0%
where the time goes in v1:
time: 40.7 us; the launch traced here: 40.2 us
  Pallas kernels  27.7 us (68%)
  local copies, waits for them, and re-layouts  10.1 us (25%)
  other arithmetic  1.74 us (4%)
  between operations  0.67 us (2%)
    pallas_call x1, Pallas kernels, kernel_exchange(): pl.pallas_call(functools.partial(kernel, dp_count, ctx_count), out_shape=...  27.7 us
    unnamed x22, local copies, waits for them, and re-layouts  10.1 us
    broadcast_in_dim x1, other arithmetic, on_device(): g_values[None]  1.02 us

profile of v1, /device:TPU:0, one launch (start us, length us, event | category | flops | bytes accessed | tf_op | source)
XLA Modules:
  0.0 40.2 jit_solution(13133006616513799829)
XLA Ops:
  0.6 0.0 copy-start
  0.6 0.9 %copy-done = bf16[1,512,128]{2,1,0:T(8,128)(2,1)S(1)} copy-done((bf16[1,512,128]{2,1,0:T(8,128)(2,1)S(1)}, bf16[1,512,128]{2,1,0:T(8,128)(2,1)}, u32[]{:S(2)}) %copy-start) | copy-done | bytes 131096
  1.5 0.0 copy-start.1
  1.5 0.9 %copy-done.1 = bf16[1,512,128]{2,1,0:T(8,128)(2,1)S(1)} copy-done((bf16[1,512,128]{2,1,0:T(8,128)(2,1)S(1)}, bf16[1,512,128]{2,1,0:T(8,128)(2,1)}, u32[]{:S(2)}) %copy-start.1) | copy-done | bytes 131096
  2.4 0.0 copy-start.2
  2.4 0.9 %copy-done.2 = bf16[1,512,128]{2,1,0:T(8,128)(2,1)S(1)} copy-done((bf16[1,512,128]{2,1,0:T(8,128)(2,1)S(1)}, bf16[1,512,128]{2,1,0:T(8,128)(2,1)}, u32[]{:S(2)}) %copy-start.2) | copy-done | bytes 131096
  3.3 0.0 copy-start.3
  3.3 0.9 %copy-done.3 = bf16[1,512,128]{2,1,0:T(8,128)(2,1)S(1)} copy-done((bf16[1,512,128]{2,1,0:T(8,128)(2,1)S(1)}, bf16[1,512,128]{2,1,0:T(8,128)(2,1)}, u32[]{:S(2)}) %copy-start.3) | copy-done | bytes 131096
  4.3 0.0 copy-start.4
  4.3 0.9 %copy-done.4 = bf16[512,128]{1,0:T(8,128)(2,1)S(1)} copy-done((bf16[512,128]{1,0:T(8,128)(2,1)S(1)}, bf16[512,128]{1,0:T(8,128)(2,1)}, u32[]{:S(2)}) %copy-start.4) | copy-done | bytes 131096
  5.2 0.0 copy-start.5
  5.2 1.0 %copy-done.5 = bf16[2,512,256]{2,1,0:T(8,128)(2,1)S(1)} copy-done((bf16[2,512,256]{2,1,0:T(8,128)(2,1)S(1)}, bf16[2,512,256]{2,1,0:T(8,128)(2,1)}, u32[]{:S(2)}) %copy-start.5) | copy-done | bytes 524312
  6.2 0.0 copy-start.6
  6.2 1.0 %copy-done.6 = bf16[2,256,512]{2,1,0:T(8,128)(2,1)S(1)} copy-done((bf16[2,256,512]{2,1,0:T(8,128)(2,1)S(1)}, bf16[2,256,512]{2,1,0:T(8,128)(2,1)}, u32[]{:S(2)}) %copy-start.6) | copy-done | bytes 524312
  7.2 0.0 copy-start.7
  7.2 0.9 %copy-done.7 = bf16[2,256,256]{2,1,0:T(8,128)(2,1)S(1)} copy-done((bf16[2,256,256]{2,1,0:T(8,128)(2,1)S(1)}, bf16[2,256,256]{2,1,0:T(8,128)(2,1)}, u32[]{:S(2)}) %copy-start.7) | copy-done | bytes 262168
  8.2 0.0 copy-start.8
  8.2 0.9 %copy-done.8 = bf16[2,256,256]{2,1,0:T(8,128)(2,1)S(1)} copy-done((bf16[2,256,256]{2,1,0:T(8,128)(2,1)S(1)}, bf16[2,256,256]{2,1,0:T(8,128)(2,1)}, u32[]{:S(2)}) %copy-start.8) | copy-done | bytes 262168
  9.1 0.0 copy-start.9
  9.1 0.9 %copy-done.9 = f32[2,256,128]{2,1,0:T(8,128)S(1)} copy-done((f32[2,256,128]{2,1,0:T(8,128)S(1)}, f32[2,256,128]{2,1,0:T(8,128)}, u32[]{:S(2)}) %copy-start.9) | copy-done | bytes 262168
  10.1 27.7 %shard_map.146 = (bf16[512,128]{1,0:T(8,128)(2,1)S(1)}, bf16[512,128]{1,0:T(8,128)(2,1)S(1)}, bf16[512,128]{1,0:T(8,128)(2,1)S(1)}) custom-call(bf16[512,128]{1,0:T(8,128)(2,1)S(1)} %bitcast.24, bf16[512,128]{1,0:T(8,128)(2,1)S(1)} %bitcast.25, bf16[512,128]{1,0:T(8,128)(2,1)S(1)} %bitcast.26, bf16[512,128]{1,0:T(8,128)(2,1)S(1)} %bitcast.27, ...), custom_call_target="tpu_custom_call" | custom-call | flops 2000000000 | bytes 4000000 | tf_op jit(solution)/shard_map/pallas_call | solution.py:356
  37.8 0.0 copy-start.10
  37.8 0.7 %copy-done.10 = f32[512]{0:T(512)S(1)} copy-done((f32[512]{0:T(512)S(1)}, f32[512]{0:T(512)}, u32[]{:S(2)}) %copy-start.10) | copy-done | bytes 2072
  38.5 1.0 %fusion.8 = (bf16[1,512,128]{2,1,0:T(8,128)(2,1)}, bf16[1,512,128]{2,1,0:T(8,128)(2,1)}, bf16[1,512,128]{2,1,0:T(8,128)(2,1)}, bf16[1,512,128]{2,1,0:T(8,128)(2,1)}) fusion(bf16[512,128]{1,0:T(8,128)(2,1)S(1)} %get-tuple-element.9, f32[512]{0:T(512)S(1)} %copy-done.10, bf16[1,512,128]{2,1,0:T(8,128)(2,1)S(1)} %copy-done.3, ...), kind=kLoop, calls=%fused_computation.16 | loop fusion | flops 1572864 | bytes 1312768 | tf_op jit(solution)/shard_map/broadcast_in_dim | solution.py:396
  39.5 0.7 %convert_element_type.63 = f32[512,128]{1,0:T(8,128)} convert(bf16[512,128]{1,0:T(8,128)(2,1)S(1)} %get-tuple-element.10) | non-fusion elementwise | flops 65536 | bytes 393216 | tf_op jit(solution)/shard_map/convert_element_type | solution.py:396
Async XLA Ops:
  0.6 0.9 %copy-start = (bf16[1,512,128]{2,1,0:T(8,128)(2,1)S(1)}, bf16[1,512,128]{2,1,0:T(8,128)(2,1)}, u32[]{:S(2)}) copy-start(bf16[1,512,128]{2,1,0:T(8,128)(2,1)} %param.11) | copy-start | bytes 393220
  1.5 0.9 %copy-start.1 = (bf16[1,512,128]{2,1,0:T(8,128)(2,1)S(1)}, bf16[1,512,128]{2,1,0:T(8,128)(2,1)}, u32[]{:S(2)}) copy-start(bf16[1,512,128]{2,1,0:T(8,128)(2,1)} %param.12) | copy-start | bytes 393220
  2.4 0.9 %copy-start.2 = (bf16[1,512,128]{2,1,0:T(8,128)(2,1)S(1)}, bf16[1,512,128]{2,1,0:T(8,128)(2,1)}, u32[]{:S(2)}) copy-start(bf16[1,512,128]{2,1,0:T(8,128)(2,1)} %param.13) | copy-start | bytes 393220
  3.3 0.9 %copy-start.3 = (bf16[1,512,128]{2,1,0:T(8,128)(2,1)S(1)}, bf16[1,512,128]{2,1,0:T(8,128)(2,1)}, u32[]{:S(2)}) copy-start(bf16[1,512,128]{2,1,0:T(8,128)(2,1)} %param.14) | copy-start | bytes 393220
  4.3 0.9 %copy-start.4 = (bf16[512,128]{1,0:T(8,128)(2,1)S(1)}, bf16[512,128]{1,0:T(8,128)(2,1)}, u32[]{:S(2)}) copy-start(bf16[512,128]{1,0:T(8,128)(2,1)} %taps_ref.1) | copy-start | bytes 393220
  5.2 1.0 %copy-start.5 = (bf16[2,512,256]{2,1,0:T(8,128)(2,1)S(1)}, bf16[2,512,256]{2,1,0:T(8,128)(2,1)}, u32[]{:S(2)}) copy-start(bf16[2,512,256]{2,1,0:T(8,128)(2,1)} %constant.10.clone.outer_f_hbm) | copy-start | bytes 1572868
  6.2 1.0 %copy-start.6 = (bf16[2,256,512]{2,1,0:T(8,128)(2,1)S(1)}, bf16[2,256,512]{2,1,0:T(8,128)(2,1)}, u32[]{:S(2)}) copy-start(bf16[2,256,512]{2,1,0:T(8,128)(2,1)} %constant.11.clone.outer_i_hbm) | copy-start | bytes 1572868
  7.2 0.9 %copy-start.7 = (bf16[2,256,256]{2,1,0:T(8,128)(2,1)S(1)}, bf16[2,256,256]{2,1,0:T(8,128)(2,1)}, u32[]{:S(2)}) copy-start(bf16[2,256,256]{2,1,0:T(8,128)(2,1)} %constant.12.clone.inner_f_hbm) | copy-start | bytes 786436
  8.2 0.9 %copy-start.8 = (bf16[2,256,256]{2,1,0:T(8,128)(2,1)S(1)}, bf16[2,256,256]{2,1,0:T(8,128)(2,1)}, u32[]{:S(2)}) copy-start(bf16[2,256,256]{2,1,0:T(8,128)(2,1)} %constant.13.clone.inner_i_hbm) | copy-start | bytes 786436
  9.1 0.9 %copy-start.9 = (f32[2,256,128]{2,1,0:T(8,128)S(1)}, f32[2,256,128]{2,1,0:T(8,128)}, u32[]{:S(2)}) copy-start(f32[2,256,128]{2,1,0:T(8,128)} %constant.14.clone.tw_hbm) | copy-start | bytes 786436
  37.8 0.7 %copy-start.10 = (f32[512]{0:T(512)S(1)}, f32[512]{0:T(512)}, u32[]{:S(2)}) copy-start(f32[512]{0:T(512)} %param.16) | copy-start | bytes 6148

commit v2 on v1

--- a/solution.py
+++ b/solution.py
@@ -142,11 +142,11 @@
 def kernel(
     dp_count,
     ctx_count,
-    outer_ref,
-    inner_ref,
-    values_ref,
-    cotan_ref,
-    taps_ref,
+    outer_hbm,
+    inner_hbm,
+    values_hbm,
+    cotan_hbm,
+    taps_hbm,
     outer_f_hbm,
     outer_i_hbm,
     inner_f_hbm,
@@ -155,6 +155,11 @@
     conv_out,
     back_out,
     grad_out,
+    outer_ref,
+    inner_ref,
+    values_ref,
+    cotan_ref,
+    taps_ref,
     mixed,
     back_in,
     recv_u,
@@ -168,6 +173,7 @@
     inner_f,
     inner_i,
     tw,
+    input_sems,
     table_sems,
     send_sems,
     recv_sems,
@@ -180,6 +186,20 @@
     my_ctx = lax.axis_index("ctx")
     me = my_dp * ctx_count + my_ctx
 
+    input_copies = [
+        pltpu.make_async_copy(src, dst, input_sems.at[i])
+        for i, (src, dst) in enumerate(
+            [
+                (inner_hbm, inner_ref),
+                (values_hbm, values_ref),
+                (taps_hbm, taps_ref),
+                (cotan_hbm, cotan_ref),
+                (outer_hbm, outer_ref),
+            ]
+        )
+    ]
+    for copy in input_copies:
+        copy.start()
     barrier = pltpu.get_barrier_semaphore()
 
     def greet(i, carry):
@@ -209,6 +229,8 @@
     for copy in table_copies:
         copy.start()
 
+    for copy in input_copies:
+        copy.wait()
     mixed[...] = (inner_ref[...].astype(F32) * values_ref[...].astype(F32)).astype(BF16)
     back_in[...] = (cotan_ref[...].astype(F32) * outer_ref[...].astype(F32)).astype(BF16)
     pl.semaphore_wait(barrier, ranks - 1)
@@ -356,17 +378,19 @@
     return pl.pallas_call(
         functools.partial(kernel, dp_count, ctx_count),
         out_shape=(local, local, local),
-        in_specs=[vmem] * 5 + [anywhere] * 5,
+        in_specs=[anywhere] * 10,
         out_specs=(vmem, vmem, vmem),
-        scratch_shapes=[signal, signal, signal, signal, one, signal, signal, one]
+        scratch_shapes=[signal] * 5
+        + [signal, signal, signal, signal, one, signal, signal, one]
         + [pltpu.VMEM(t.shape, t.dtype) for t in constants]
         + [
+            pltpu.SemaphoreType.DMA((5,)),
             pltpu.SemaphoreType.DMA((5,)),
             pltpu.SemaphoreType.DMA((6,)),
             pltpu.SemaphoreType.DMA((6,)),
         ],
         compiler_params=pltpu.CompilerParams(
-            collective_id=0, has_side_effects=True, vmem_limit_bytes=48 * 1024 * 1024
+            collective_id=0, has_side_effects=True, vmem_limit_bytes=60 * 1024 * 1024
         ),
         cost_estimate=pl.CostEstimate(
             flops=2_000_000_000, bytes_accessed=4_000_000, transcendentals=0

time: 40.7 us -> 33.2 us (0.82)
  local copies, waits for them, and re-layouts: 10.1 us -> 0.66 us
  Pallas kernels: 27.7 us -> 28.9 us
  other arithmetic: 1.74 us -> 2.75 us
    unnamed x22 -> x12, local copies, waits for them, and re-layouts: 10.1 us -> 0.66 us
    pallas_call x1, Pallas kernels: 27.7 us -> 28.9 us  [kernel_exchange(): pl.pallas_call(functools.partial(kernel, dp_count, ctx_count), out_shape=...]
    broadcast_in_dim x1, other arithmetic: 1.02 us -> 2.03 us  [on_device(): g_values[None]]
where the time goes in v2:
time: 33.2 us; the launch traced here: 33 us
  Pallas kernels  28.9 us (87%)
  other arithmetic  2.75 us (8%)
  between operations  0.71 us (2%)
  local copies, waits for them, and re-layouts  0.66 us (2%)
    pallas_call x1, Pallas kernels, kernel_exchange(): pl.pallas_call(functools.partial(kernel, dp_count, ctx_count), out_shape=...  28.9 us
    broadcast_in_dim x1, other arithmetic, on_device(): g_values[None]  2.03 us
    convert_element_type x1, other arithmetic, on_device(): filter_grad.astype(F32)  0.72 us

profile of v2, /device:TPU:0, one launch (start us, length us, event | category | flops | bytes accessed | tf_op | source)
XLA Modules:
  0.0 33.0 jit_solution(7926907570277792276)
XLA Ops:
  0.6 0.0 copy-start
  0.6 0.0 copy-start.1
  0.7 0.0 copy-start.2
  0.7 0.0 copy-start.3
  0.7 28.9 %shard_map.146 = (bf16[512,128]{1,0:T(8,128)(2,1)}, bf16[512,128]{1,0:T(8,128)(2,1)}, bf16[512,128]{1,0:T(8,128)(2,1)}) custom-call(bf16[512,128]{1,0:T(8,128)(2,1)} %bitcast.24, bf16[512,128]{1,0:T(8,128)(2,1)} %bitcast.25, bf16[512,128]{1,0:T(8,128)(2,1)} %bitcast.26, bf16[512,128]{1,0:T(8,128)(2,1)} %bitcast.27, bf16[512,128]{1,0:T(8,128)(2,1)} %taps_hbm.1, ...), custom_call_target="tpu_custom_call" | custom-call | flops 2000000000 | bytes 4000000 | tf_op jit(solution)/shard_map/pallas_call | solution.py:378
  29.5 0.0 copy-start.5
  29.6 0.0 copy-done
  29.6 0.0 copy-done.1
  29.6 0.0 copy-done.2
  29.6 0.0 copy-done.3
  29.6 0.6 %copy-done.5 = f32[512]{0:T(512)S(1)} copy-done((f32[512]{0:T(512)S(1)}, f32[512]{0:T(512)}, u32[]{:S(2)}) %copy-start.5) | copy-done | bytes 2072
  30.2 0.0 copy-start.4
  30.2 2.0 %fusion.8 = (bf16[1,512,128]{2,1,0:T(8,128)(2,1)}, bf16[1,512,128]{2,1,0:T(8,128)(2,1)}, bf16[1,512,128]{2,1,0:T(8,128)(2,1)}, bf16[1,512,128]{2,1,0:T(8,128)(2,1)}) fusion(bf16[512,128]{1,0:T(8,128)(2,1)} %get-tuple-element.9, f32[512]{0:T(512)S(1)} %copy-done.5, bf16[1,512,128]{2,1,0:T(8,128)(2,1)S(1)} %copy-done.3, bf16[1,512,128]{2,1,0:T(8,128)(2,1)S(1)} %copy-done.1, ...), kind=kLoop, calls=%fused_computation.16 | loop fusion | flops 1572864 | bytes 1312768 | tf_op jit(solution)/shard_map/broadcast_in_dim | solution.py:420
  32.3 0.0 copy-done.4
  32.3 0.7 %convert_element_type.63 = f32[512,128]{1,0:T(8,128)} convert(bf16[512,128]{1,0:T(8,128)(2,1)S(1)} %copy-done.4) | non-fusion elementwise | flops 65536 | bytes 393216 | tf_op jit(solution)/shard_map/convert_element_type | solution.py:420
Async XLA Ops:
  0.6 28.9 %copy-start = (bf16[1,512,128]{2,1,0:T(8,128)(2,1)S(1)}, bf16[1,512,128]{2,1,0:T(8,128)(2,1)}, u32[]{:S(2)}) copy-start(bf16[1,512,128]{2,1,0:T(8,128)(2,1)} %param.11) | copy-start | bytes 393220
  0.6 28.9 %copy-start.1 = (bf16[1,512,128]{2,1,0:T(8,128)(2,1)S(1)}, bf16[1,512,128]{2,1,0:T(8,128)(2,1)}, u32[]{:S(2)}) copy-start(bf16[1,512,128]{2,1,0:T(8,128)(2,1)} %param.12) | copy-start | bytes 393220
  0.7 28.9 %copy-start.2 = (bf16[1,512,128]{2,1,0:T(8,128)(2,1)S(1)}, bf16[1,512,128]{2,1,0:T(8,128)(2,1)}, u32[]{:S(2)}) copy-start(bf16[1,512,128]{2,1,0:T(8,128)(2,1)} %param.13) | copy-start | bytes 393220
  0.7 28.9 %copy-start.3 = (bf16[1,512,128]{2,1,0:T(8,128)(2,1)S(1)}, bf16[1,512,128]{2,1,0:T(8,128)(2,1)}, u32[]{:S(2)}) copy-start(bf16[1,512,128]{2,1,0:T(8,128)(2,1)} %param.14) | copy-start | bytes 393220
  29.5 0.7 %copy-start.5 = (f32[512]{0:T(512)S(1)}, f32[512]{0:T(512)}, u32[]{:S(2)}) copy-start(f32[512]{0:T(512)} %param.16) | copy-start | bytes 6148
  30.2 2.0 %copy-start.4 = (bf16[512,128]{1,0:T(8,128)(2,1)S(1)}, bf16[512,128]{1,0:T(8,128)(2,1)}, u32[]{:S(2)}) copy-start(bf16[512,128]{1,0:T(8,128)(2,1)} %get-tuple-element.10) | copy-start | bytes 393220

commit v3 on v2

--- a/solution.py
+++ b/solution.py
@@ -105,10 +105,8 @@
     return conv_seq, back_seq, filter_grad
 
 
-def two_parts(table):
-    high = table.astype(np.float32).astype(BF16)
-    low = (table - high.astype(np.float64)).astype(np.float32).astype(BF16)
-    return np.stack([np.asarray(high), np.asarray(low)])
+def rounded(table):
+    return np.asarray(table.astype(np.float32).astype(BF16))
 
 
 @functools.lru_cache(maxsize=None)
@@ -127,16 +125,11 @@
     angle_tw = 2.0 * np.pi * np.outer(2 * n + 1, m) / (2.0 * total)
     tw = np.stack([np.cos(angle_tw), np.sin(angle_tw)])
     tw = np.repeat(tw, group, axis=1).astype(np.float32)
-    return two_parts(outer_f), two_parts(outer_i), two_parts(inner_f), two_parts(inner_i), tw
+    return rounded(outer_f), rounded(outer_i), rounded(inner_f), rounded(inner_i), tw
 
 
 def dot(a, b):
     return jnp.dot(a, b, preferred_element_type=F32)
-
-
-def split(x):
-    high = x.astype(BF16)
-    return high, (x - high.astype(F32)).astype(BF16)
 
 
 def kernel(
@@ -152,22 +145,22 @@
     inner_f_hbm,
     inner_i_hbm,
     tw_hbm,
-    conv_out,
-    back_out,
+    gain_hbm,
+    state_out,
+    g_mixed_out,
     grad_out,
     outer_ref,
     inner_ref,
     values_ref,
     cotan_ref,
     taps_ref,
-    mixed,
-    back_in,
-    recv_u,
-    recv_d,
+    pair,
+    recv_pair,
     recv_h,
-    sent_conv,
-    sent_back,
+    sent_pair,
+    result_pair,
     sent_grad,
+    gain_ref,
     outer_f,
     outer_i,
     inner_f,
@@ -179,7 +172,7 @@
     recv_sems,
 ):
     ranks = dp_count * ctx_count
-    chans, width = mixed.shape
+    chans, width = taps_ref.shape
     group = chans // ranks
     rows = ctx_count * group
     my_dp = lax.axis_index("dp")
@@ -223,6 +216,7 @@
                 (tw_hbm, tw),
                 (inner_i_hbm, inner_i),
                 (outer_i_hbm, outer_i),
+                (gain_hbm, gain_ref),
             ]
         )
     ]
@@ -231,8 +225,15 @@
 
     for copy in input_copies:
         copy.wait()
-    mixed[...] = (inner_ref[...].astype(F32) * values_ref[...].astype(F32)).astype(BF16)
-    back_in[...] = (cotan_ref[...].astype(F32) * outer_ref[...].astype(F32)).astype(BF16)
+    def by_peer(x):
+        return x.reshape(ranks, group, width)
+
+    pair[:, :group] = by_peer(
+        (inner_ref[...].astype(F32) * values_ref[...].astype(F32)).astype(BF16)
+    )
+    pair[:, group:] = by_peer(
+        (cotan_ref[...].astype(F32) * outer_ref[...].astype(F32)).astype(BF16)
+    )
     pl.semaphore_wait(barrier, ranks - 1)
 
     def chunk(ref, index):
@@ -248,28 +249,35 @@
             device_id_type=MESH,
         )
 
+    def target(step):
+        pair = step // dp_count
+        half = (pair + 1) // 2
+        sign = 1 - 2 * lax.rem(pair + 1, 2)
+        ctx = lax.rem(my_ctx + ctx_count // 2 + sign * half + ctx_count, ctx_count)
+        dp = lax.rem(my_dp + lax.rem(step, dp_count) + 1, dp_count)
+        return dp, ctx
+
     def send_taps(i, carry):
-        ctx = lax.rem(my_ctx + i, ctx_count)
+        half = (i + 1) // 2
+        sign = 1 - 2 * lax.rem(i + 1, 2)
+        ctx = lax.rem(my_ctx + ctx_count // 2 + sign * half + ctx_count, ctx_count)
         peer = my_dp * ctx_count + ctx
         to_peer(chunk(taps_ref, peer), chunk(recv_h, my_ctx), 0, peer).start()
         return carry
 
-    def send_mixed(i, carry):
-        peer = lax.rem(me + i, ranks)
-        to_peer(chunk(mixed, peer), chunk(recv_u, me), 1, peer).start()
-        return carry
-
-    def send_back(i, carry):
-        peer = lax.rem(me + i, ranks)
-        to_peer(chunk(back_in, peer), chunk(recv_d, me), 2, peer).start()
-        return carry
-
-    lax.fori_loop(1, ctx_count, send_taps, 0)
-    lax.fori_loop(1, ranks, send_mixed, 0)
-    lax.fori_loop(1, ranks, send_back, 0)
+    def send_pairs(src, dst, which):
+        def step(i, carry):
+            dp, ctx = target(i)
+            peer = dp * ctx_count + ctx
+            to_peer(src.at[peer], dst.at[me], which, peer).start()
+            return carry
+
+        lax.fori_loop(0, ranks - 1, step, 0)
+        pltpu.make_async_copy(src.at[me], dst.at[me], recv_sems.at[which]).start()
+
+    send_pairs(pair, recv_pair, 1)
+    lax.fori_loop(0, ctx_count - 1, send_taps, 0)
     pltpu.make_async_copy(chunk(taps_ref, me), chunk(recv_h, my_ctx), recv_sems.at[0]).start()
-    pltpu.make_async_copy(chunk(mixed, me), chunk(recv_u, me), recv_sems.at[1]).start()
-    pltpu.make_async_copy(chunk(back_in, me), chunk(recv_d, me), recv_sems.at[2]).start()
 
     def arrived(ref, which):
         pltpu.make_async_copy(ref, ref, recv_sems.at[which]).wait()
@@ -277,7 +285,7 @@
     def spectra(signals):
         count = len(signals)
         side = jnp.concatenate(signals, axis=1)
-        a = dot(outer_f[0], side) + dot(outer_f[1], side)
+        a = dot(outer_f[...], side)
         parts = []
         for s in range(count):
             re = a[:rows, s * width : (s + 1) * width]
@@ -285,8 +293,7 @@
             parts.append(
                 jnp.concatenate([re * tw[0] + im * tw[1], im * tw[0] - re * tw[1]], axis=1)
             )
-        high, low = split(jnp.concatenate(parts, axis=0))
-        x = dot(high, inner_f[0]) + (dot(high, inner_f[1]) + dot(low, inner_f[0]))
+        x = dot(jnp.concatenate(parts, axis=0).astype(BF16), inner_f[...])
         return [
             (x[s * rows : (s + 1) * rows, :width], x[s * rows : (s + 1) * rows, width:])
             for s in range(count)
@@ -294,10 +301,8 @@
 
     def signals_of(products):
         count = len(products)
-        high, low = split(
-            jnp.concatenate([jnp.concatenate([re, im], axis=1) for re, im in products], axis=0)
-        )
-        z = dot(high, inner_i[0]) + (dot(high, inner_i[1]) + dot(low, inner_i[0]))
+        side = jnp.concatenate([jnp.concatenate([re, im], axis=1) for re, im in products], axis=0)
+        z = dot(side.astype(BF16), inner_i[...])
         parts = []
         for s in range(count):
             re = z[s * rows : (s + 1) * rows, :width]
@@ -305,8 +310,7 @@
             parts.append(
                 jnp.concatenate([re * tw[0] - im * tw[1], im * tw[0] + re * tw[1]], axis=0)
             )
-        high, low = split(jnp.concatenate(parts, axis=1))
-        y = dot(outer_i[0], high) + (dot(outer_i[1], high) + dot(outer_i[0], low))
+        y = dot(outer_i[...], jnp.concatenate(parts, axis=1).astype(BF16))
         return [y[:, s * width : (s + 1) * width] for s in range(count)]
 
     def times(a, b):
@@ -315,55 +319,77 @@
     def times_conj(a, b):
         return a[0] * b[0] + a[1] * b[1], a[1] * b[0] - a[0] * b[1]
 
-    def return_sequences(src, dst, which):
-        def step(i, carry):
-            peer = lax.rem(me + i, ranks)
-            to_peer(chunk(src, peer), chunk(dst, me), which, peer).start()
-            return carry
-
-        lax.fori_loop(1, ranks, step, 0)
-        pltpu.make_async_copy(chunk(src, me), chunk(dst, me), recv_sems.at[which]).start()
-
-    arrived(recv_h, 0)
-    arrived(recv_u, 1)
+    def sequence(s, part):
+        block = recv_pair[s * ctx_count : (s + 1) * ctx_count, part * group : (part + 1) * group]
+        return block.reshape(rows, width)
+
+    def keep(s, part, y):
+        sent_pair[s * ctx_count : (s + 1) * ctx_count, part * group : (part + 1) * group] = (
+            y.astype(BF16).reshape(ctx_count, group, width)
+        )
+
+    arrived(recv_pair, 1)
     for copy in table_copies:
         copy.wait()
-    spec = spectra(
-        [recv_h[...]] + [recv_u[s * rows : (s + 1) * rows] for s in range(dp_count)]
-    )
-    spec_h, spec_u = spec[0], spec[1:]
-    for s, y in enumerate(signals_of([times(u, spec_h) for u in spec_u])):
-        sent_conv[s * rows : (s + 1) * rows] = y.astype(BF16)
-    return_sequences(sent_conv, conv_out, 3)
-
-    arrived(recv_d, 2)
-    spec_d = spectra([recv_d[s * rows : (s + 1) * rows] for s in range(dp_count)])
-    for s, y in enumerate(signals_of([times_conj(d, spec_h) for d in spec_d])):
-        sent_back[s * rows : (s + 1) * rows] = y.astype(BF16)
-    return_sequences(sent_back, back_out, 4)
-
+    spec_u = spectra([sequence(s, 0) for s in range(dp_count)])
+    spec_d = spectra([sequence(s, 1) for s in range(dp_count)])
     terms = [times_conj(d, u) for d, u in zip(spec_d, spec_u)]
     term = (sum(t[0] for t in terms), sum(t[1] for t in terms))
     norm_scale = 1.0 / math.sqrt(dp_count * ctx_count * width)
     sent_grad[...] = (signals_of([term])[0] * norm_scale).astype(BF16)
 
     def send_grad(i, carry):
-        peer = lax.rem(me + i, ranks)
-        to_peer(chunk(sent_grad, lax.rem(peer, ctx_count)), chunk(grad_out, me), 5, peer).start()
+        half = (i + 1) // 2
+        sign = 1 - 2 * lax.rem(i + 1, 2)
+        ctx = lax.rem(my_ctx + ctx_count // 2 + sign * half + ctx_count, ctx_count)
+        peer = my_dp * ctx_count + ctx
+        to_peer(chunk(sent_grad, ctx), chunk(grad_out, me), 3, peer).start()
         return carry
 
-    lax.fori_loop(1, ranks, send_grad, 0)
-    pltpu.make_async_copy(chunk(sent_grad, my_ctx), chunk(grad_out, me), recv_sems.at[5]).start()
-
-    arrived(conv_out, 3)
-    arrived(back_out, 4)
-    arrived(grad_out, 5)
-    for which, count in ((0, ctx_count), (1, ranks), (2, ranks), (3, ranks), (4, ranks), (5, ranks)):
-        part = mixed.at[pl.ds(0, (count - 1) * group)]
+    lax.fori_loop(0, ctx_count - 1, send_grad, 0)
+    pltpu.make_async_copy(chunk(sent_grad, my_ctx), chunk(grad_out, me), recv_sems.at[3]).start()
+
+    arrived(recv_h, 0)
+    spec_h = spectra([recv_h[...]])[0]
+    for s, y in enumerate(signals_of([times(u, spec_h) for u in spec_u])):
+        keep(s, 0, y)
+    for s, y in enumerate(signals_of([times_conj(d, spec_h) for d in spec_d])):
+        keep(s, 1, y)
+    send_pairs(sent_pair, result_pair, 2)
+    def share(ref, dp):
+        return ref.at[pl.ds(pl.multiple_of(dp * rows, rows), rows)]
+
+    mine = share(grad_out, my_dp)
+    arrived(mine, 3)
+    forwards = [
+        to_peer(mine, mine, 3 + i, lax.rem(my_dp + i, dp_count) * ctx_count + my_ctx)
+        for i in range(1, dp_count)
+    ]
+    for copy in forwards:
+        copy.start()
+
+    per = width // group
+
+    def gain_of(t):
+        return jnp.broadcast_to(gain_ref[t * width : (t + 1) * width][None, :], (width, width)).T
+
+    arrived(result_pair, 2)
+    for t in range(chans // width):
+        gain = gain_of(t)
+        for part, out in ((0, state_out), (1, g_mixed_out)):
+            which = (slice(t * per, (t + 1) * per), slice(part * group, (part + 1) * group))
+            signal = pair[which].reshape(width, width).astype(F32)
+            result = result_pair[which].reshape(width, width).astype(F32)
+            out[t * width : (t + 1) * width] = result + gain * signal
+    for copy in forwards:
+        copy.wait()
+    taps_sent = taps_ref.at[pl.ds(0, (ctx_count - 1) * group)]
+    pairs_sent = pair.at[pl.ds(0, ranks - 1)]
+    for which, part in ((0, taps_sent), (1, pairs_sent), (2, pairs_sent), (3, taps_sent)):
         pltpu.make_async_copy(part, part, send_sems.at[which]).wait()
 
 
-def kernel_exchange(outer, inner, values, cotan, filter_taps):
+def kernel_layer(outer, inner, values, cotan, filter_taps, gain):
     ctx_count = lax.axis_size("ctx")
     dp_count = lax.axis_size("dp")
     chans, width = outer.shape
@@ -375,19 +401,21 @@
     local = jax.ShapeDtypeStruct((chans, width), BF16)
     signal = pltpu.VMEM((chans, width), BF16)
     one = pltpu.VMEM((rows, width), BF16)
+    pair = pltpu.VMEM((dp_count * ctx_count, 2 * group, width), BF16)
+    wide = jax.ShapeDtypeStruct((chans, width), F32)
     return pl.pallas_call(
         functools.partial(kernel, dp_count, ctx_count),
-        out_shape=(local, local, local),
-        in_specs=[anywhere] * 10,
+        out_shape=(wide, wide, local),
+        in_specs=[anywhere] * 11,
         out_specs=(vmem, vmem, vmem),
         scratch_shapes=[signal] * 5
-        + [signal, signal, signal, signal, one, signal, signal, one]
+        + [pair, pair, one, pair, pair, one, pltpu.VMEM((chans,), F32)]
         + [pltpu.VMEM(t.shape, t.dtype) for t in constants]
         + [
             pltpu.SemaphoreType.DMA((5,)),
-            pltpu.SemaphoreType.DMA((5,)),
             pltpu.SemaphoreType.DMA((6,)),
-            pltpu.SemaphoreType.DMA((6,)),
+            pltpu.SemaphoreType.DMA((3 + dp_count,)),
+            pltpu.SemaphoreType.DMA((3 + dp_count,)),
         ],
         compiler_params=pltpu.CompilerParams(
             collective_id=0, has_side_effects=True, vmem_limit_bytes=60 * 1024 * 1024
@@ -395,7 +423,7 @@
         cost_estimate=pl.CostEstimate(
             flops=2_000_000_000, bytes_accessed=4_000_000, transcendentals=0
         ),
-    )(outer, inner, values, cotan, filter_taps, *[jnp.asarray(t) for t in constants])
+    )(outer, inner, values, cotan, filter_taps, *[jnp.asarray(t) for t in constants], gain)
 
 
 def on_device(gate_outer, gate_inner, values_in, cotangent, filter_taps, skip_gain):
@@ -404,17 +432,20 @@
     values = values_in[0]
     cotan = cotangent[0]
     ranks = lax.axis_size("ctx") * lax.axis_size("dp")
-    mixed = (inner.astype(F32) * values.astype(F32)).astype(BF16)
-    back_in = (cotan.astype(F32) * outer.astype(F32)).astype(BF16)
-    if outer.shape[0] % (16 * ranks) == 0 and outer.shape[1] == inner_order:
-        conv_seq, back_seq, filter_grad = kernel_exchange(outer, inner, values, cotan, filter_taps)
+    chans, width = outer.shape
+    if chans % (16 * ranks) == 0 and chans % width == 0 and width == inner_order:
+        state, g_mixed, filter_grad = kernel_layer(
+            outer, inner, values, cotan, filter_taps, skip_gain
+        )
     else:
+        mixed = (inner.astype(F32) * values.astype(F32)).astype(BF16)
+        back_in = (cotan.astype(F32) * outer.astype(F32)).astype(BF16)
         conv_seq, back_seq, filter_grad = general_exchange(mixed, back_in, filter_taps)
-    gain = skip_gain[:, None]
-    state = conv_seq.astype(F32) + gain * mixed.astype(F32)
+        gain = skip_gain[:, None]
+        state = conv_seq.astype(F32) + gain * mixed.astype(F32)
+        g_mixed = back_seq.astype(F32) + gain * back_in.astype(F32)
     layer = (outer.astype(F32) * state).astype(BF16)
     g_outer = (cotan.astype(F32) * state).astype(BF16)
-    g_mixed = back_seq.astype(F32) + gain * back_in.astype(F32)
     g_inner = (g_mixed * values.astype(F32)).astype(BF16)
     g_values = (g_mixed * inner.astype(F32)).astype(BF16)
     return (layer[None], g_outer[None], g_inner[None], g_values[None], filter_grad.astype(F32))

time: 33.2 us -> 30.5 us (0.919)
  Pallas kernels: 28.9 us -> 27 us
  local copies, waits for them, and re-layouts: 0.66 us -> 0.02 us
    pallas_call x1, Pallas kernels: 28.9 us -> 27 us  [kernel_layer(): pl.pallas_call(functools.partial(kernel, dp_count, ctx_count), out_shape=...]
    unnamed x12 -> x10, local copies, waits for them, and re-layouts: 0.66 us -> 0.02 us
where the time goes in v3:
time: 30.5 us; the launch traced here: 30.3 us
  Pallas kernels  27 us (89%)
  other arithmetic  2.63 us (9%)
  between operations  0.71 us (2%)
    pallas_call x1, Pallas kernels, kernel_layer(): pl.pallas_call(functools.partial(kernel, dp_count, ctx_count), out_shape=...  27 us
    broadcast_in_dim x1, other arithmetic, on_device(): g_outer[None]  1.91 us
    convert_element_type x1, other arithmetic, on_device(): filter_grad.astype(F32)  0.72 us

profile of v3, /device:TPU:0, one launch (start us, length us, event | category | flops | bytes accessed | tf_op | source)
XLA Modules:
  0.0 30.3 jit_solution(15860100014710422239)
XLA Ops:
  0.6 0.0 copy-start
  0.6 0.0 copy-start.1
  0.7 0.0 copy-start.2
  0.7 0.0 copy-start.3
  0.7 27.0 %shard_map.146 = (f32[512,128]{1,0:T(8,128)}, f32[512,128]{1,0:T(8,128)}, bf16[512,128]{1,0:T(8,128)(2,1)}) custom-call(bf16[512,128]{1,0:T(8,128)(2,1)} %bitcast.16, bf16[512,128]{1,0:T(8,128)(2,1)} %bitcast.17, bf16[512,128]{1,0:T(8,128)(2,1)} %bitcast.18, bf16[512,128]{1,0:T(8,128)(2,1)} %bitcast.19, bf16[512,128]{1,0:T(8,128)(2,1)} %taps_hbm.1, ...), custom_call_target="tpu_custom_call" | custom-call | flops 2000000000 | bytes 4000000 | tf_op jit(solution)/shard_map/pallas_call | solution.py:406
  27.6 0.0 copy-done
  27.7 0.0 copy-done.1
  27.7 0.0 copy-done.2
  27.7 0.0 copy-done.3
  27.7 0.0 copy-start.4
  27.7 1.9 %fusion.1 = (bf16[1,512,128]{2,1,0:T(8,128)(2,1)}, bf16[1,512,128]{2,1,0:T(8,128)(2,1)}, bf16[1,512,128]{2,1,0:T(8,128)(2,1)}, bf16[1,512,128]{2,1,0:T(8,128)(2,1)}) fusion(f32[512,128]{1,0:T(8,128)} %get-tuple-element.8, bf16[1,512,128]{2,1,0:T(8,128)(2,1)S(1)} %copy-done.3, bf16[1,512,128]{2,1,0:T(8,128)(2,1)S(1)} %copy-done, ...), kind=kLoop, calls=%fused_computation.5 | loop fusion | flops 786432 | bytes 1572864 | tf_op jit(solution)/shard_map/broadcast_in_dim | solution.py:451
  29.6 0.0 copy-done.4
  29.6 0.7 %convert_element_type.35 = f32[512,128]{1,0:T(8,128)} convert(bf16[512,128]{1,0:T(8,128)(2,1)S(1)} %copy-done.4) | non-fusion elementwise | flops 65536 | bytes 393216 | tf_op jit(solution)/shard_map/convert_element_type | solution.py:451
Async XLA Ops:
  0.6 27.0 %copy-start = (bf16[1,512,128]{2,1,0:T(8,128)(2,1)S(1)}, bf16[1,512,128]{2,1,0:T(8,128)(2,1)}, u32[]{:S(2)}) copy-start(bf16[1,512,128]{2,1,0:T(8,128)(2,1)} %param.11) | copy-start | bytes 393220
  0.6 27.0 %copy-start.1 = (bf16[1,512,128]{2,1,0:T(8,128)(2,1)S(1)}, bf16[1,512,128]{2,1,0:T(8,128)(2,1)}, u32[]{:S(2)}) copy-start(bf16[1,512,128]{2,1,0:T(8,128)(2,1)} %param.12) | copy-start | bytes 393220
  0.7 27.0 %copy-start.2 = (bf16[1,512,128]{2,1,0:T(8,128)(2,1)S(1)}, bf16[1,512,128]{2,1,0:T(8,128)(2,1)}, u32[]{:S(2)}) copy-start(bf16[1,512,128]{2,1,0:T(8,128)(2,1)} %param.13) | copy-start | bytes 393220
  0.7 27.0 %copy-start.3 = (bf16[1,512,128]{2,1,0:T(8,128)(2,1)S(1)}, bf16[1,512,128]{2,1,0:T(8,128)(2,1)}, u32[]{:S(2)}) copy-start(bf16[1,512,128]{2,1,0:T(8,128)(2,1)} %param.14) | copy-start | bytes 393220
  27.7 1.9 %copy-start.4 = (bf16[512,128]{1,0:T(8,128)(2,1)S(1)}, bf16[512,128]{1,0:T(8,128)(2,1)}, u32[]{:S(2)}) copy-start(bf16[512,128]{1,0:T(8,128)(2,1)} %get-tuple-element.10) | copy-start | bytes 393220

commit v4 on v3

--- a/solution.py
+++ b/solution.py
@@ -331,8 +331,8 @@
     arrived(recv_pair, 1)
     for copy in table_copies:
         copy.wait()
-    spec_u = spectra([sequence(s, 0) for s in range(dp_count)])
-    spec_d = spectra([sequence(s, 1) for s in range(dp_count)])
+    spec = spectra([sequence(s, part) for part in range(2) for s in range(dp_count)])
+    spec_u, spec_d = spec[:dp_count], spec[dp_count:]
     terms = [times_conj(d, u) for d, u in zip(spec_d, spec_u)]
     term = (sum(t[0] for t in terms), sum(t[1] for t in terms))
     norm_scale = 1.0 / math.sqrt(dp_count * ctx_count * width)
@@ -351,10 +351,11 @@
 
     arrived(recv_h, 0)
     spec_h = spectra([recv_h[...]])[0]
-    for s, y in enumerate(signals_of([times(u, spec_h) for u in spec_u])):
-        keep(s, 0, y)
-    for s, y in enumerate(signals_of([times_conj(d, spec_h) for d in spec_d])):
-        keep(s, 1, y)
+    results = signals_of(
+        [times(u, spec_h) for u in spec_u] + [times_conj(d, spec_h) for d in spec_d]
+    )
+    for i, y in enumerate(results):
+        keep(i % dp_count, i // dp_count, y)
     send_pairs(sent_pair, result_pair, 2)
     def share(ref, dp):
         return ref.at[pl.ds(pl.multiple_of(dp * rows, rows), rows)]

time: 30.5 us -> 30.6 us (level)
  no operation moved by 1% of the time
where the time goes in v4:
time: 30.6 us; the launch traced here: 30.5 us
  Pallas kernels  27.1 us (89%)
  other arithmetic  2.63 us (9%)
  between operations  0.71 us (2%)
    pallas_call x1, Pallas kernels, kernel_layer(): pl.pallas_call(functools.partial(kernel, dp_count, ctx_count), out_shape=...  27.1 us
    broadcast_in_dim x1, other arithmetic, on_device(): g_outer[None]  1.91 us
    convert_element_type x1, other arithmetic, on_device(): filter_grad.astype(F32)  0.72 us

profile of v4, /device:TPU:0, one launch (start us, length us, event | category | flops | bytes accessed | tf_op | source)
XLA Modules:
  0.0 30.5 jit_solution(14305077218217040198)
XLA Ops:
  0.6 0.0 copy-start
  0.6 0.0 copy-start.1
  0.7 0.0 copy-start.2
  0.7 0.0 copy-start.3
  0.7 27.1 %shard_map.146 = (f32[512,128]{1,0:T(8,128)}, f32[512,128]{1,0:T(8,128)}, bf16[512,128]{1,0:T(8,128)(2,1)}) custom-call(bf16[512,128]{1,0:T(8,128)(2,1)} %bitcast.16, bf16[512,128]{1,0:T(8,128)(2,1)} %bitcast.17, bf16[512,128]{1,0:T(8,128)(2,1)} %bitcast.18, bf16[512,128]{1,0:T(8,128)(2,1)} %bitcast.19, bf16[512,128]{1,0:T(8,128)(2,1)} %taps_hbm.1, ...), custom_call_target="tpu_custom_call" | custom-call | flops 2000000000 | bytes 4000000 | tf_op jit(solution)/shard_map/pallas_call | solution.py:407
  27.8 0.0 copy-done
  27.8 0.0 copy-done.1
  27.8 0.0 copy-done.2
  27.8 0.0 copy-done.3
  27.8 0.0 copy-start.4
  27.8 1.9 %fusion.1 = (bf16[1,512,128]{2,1,0:T(8,128)(2,1)}, bf16[1,512,128]{2,1,0:T(8,128)(2,1)}, bf16[1,512,128]{2,1,0:T(8,128)(2,1)}, bf16[1,512,128]{2,1,0:T(8,128)(2,1)}) fusion(f32[512,128]{1,0:T(8,128)} %get-tuple-element.8, bf16[1,512,128]{2,1,0:T(8,128)(2,1)S(1)} %copy-done.3, bf16[1,512,128]{2,1,0:T(8,128)(2,1)S(1)} %copy-done, ...), kind=kLoop, calls=%fused_computation.5 | loop fusion | flops 786432 | bytes 1572864 | tf_op jit(solution)/shard_map/broadcast_in_dim | solution.py:452
  29.7 0.0 copy-done.4
  29.7 0.7 %convert_element_type.35 = f32[512,128]{1,0:T(8,128)} convert(bf16[512,128]{1,0:T(8,128)(2,1)S(1)} %copy-done.4) | non-fusion elementwise | flops 65536 | bytes 393216 | tf_op jit(solution)/shard_map/convert_element_type | solution.py:452
Async XLA Ops:
  0.6 27.1 %copy-start = (bf16[1,512,128]{2,1,0:T(8,128)(2,1)S(1)}, bf16[1,512,128]{2,1,0:T(8,128)(2,1)}, u32[]{:S(2)}) copy-start(bf16[1,512,128]{2,1,0:T(8,128)(2,1)} %param.11) | copy-start | bytes 393220
  0.6 27.1 %copy-start.1 = (bf16[1,512,128]{2,1,0:T(8,128)(2,1)S(1)}, bf16[1,512,128]{2,1,0:T(8,128)(2,1)}, u32[]{:S(2)}) copy-start(bf16[1,512,128]{2,1,0:T(8,128)(2,1)} %param.12) | copy-start | bytes 393220
  0.7 27.1 %copy-start.2 = (bf16[1,512,128]{2,1,0:T(8,128)(2,1)S(1)}, bf16[1,512,128]{2,1,0:T(8,128)(2,1)}, u32[]{:S(2)}) copy-start(bf16[1,512,128]{2,1,0:T(8,128)(2,1)} %param.13) | copy-start | bytes 393220
  0.7 27.1 %copy-start.3 = (bf16[1,512,128]{2,1,0:T(8,128)(2,1)S(1)}, bf16[1,512,128]{2,1,0:T(8,128)(2,1)}, u32[]{:S(2)}) copy-start(bf16[1,512,128]{2,1,0:T(8,128)(2,1)} %param.14) | copy-start | bytes 393220
  27.8 1.9 %copy-start.4 = (bf16[512,128]{1,0:T(8,128)(2,1)S(1)}, bf16[512,128]{1,0:T(8,128)(2,1)}, u32[]{:S(2)}) copy-start(bf16[512,128]{1,0:T(8,128)(2,1)} %get-tuple-element.10) | copy-start | bytes 393220
